TPU v7x, 32 devices: a whole 2x2x4 slice. The times are simulated.
32 devices in a mesh: dp: 4 (over z), expert: 8 (over y, x, core).
Axes of the slice: x: 2, y: 2, z: 4, core: 2. Of those that a mesh axis runs over, the one named last changes fastest.
Arguments:
- images: bfloat16 [256, 197, 384], P(('dp', 'expert')), may hold values from -6 to 6
- cotangent: bfloat16 [256, 197, 384], P(('dp', 'expert')), may hold values from -6 to 6
- router_noise: float32 [256, 197, 8], P(('dp', 'expert')), may hold values from -3 to 3
- routes: int32 [256, 197, 2], P(('dp', 'expert')), may hold values from 0 to 7, all different within a row
- seat_order: int32 [32, 3152], P(('dp', 'expert')), may hold values from 0 to 3151, each once within a row
- norm1_gain: float32 [384], replicated, may hold values from 0.5 to 1.5
- norm1_shift: float32 [384], replicated, may hold values from -1 to 1
- query_weight: bfloat16 [384, 384], replicated, may hold values from -0.3125 to 0.3125
- query_bias: float32 [384], replicated, may hold values from -1 to 1
- key_weight: bfloat16 [384, 384], replicated, may hold values from -0.3125 to 0.3125
- value_weight: bfloat16 [384, 384], replicated, may hold values from -0.3125 to 0.3125
- value_bias: float32 [384], replicated, may hold values from -1 to 1
- output_weight: bfloat16 [384, 384], replicated, may hold values from -2.5 to 2.5
- output_bias: float32 [384], replicated, may hold values from -1 to 1
- norm2_gain: float32 [384], replicated, may hold values from 0.5 to 1.5
- norm2_shift: float32 [384], replicated, may hold values from -1 to 1
- router_weight: bfloat16 [384, 8], replicated, may hold values from -0.1796875 to 0.1796875
- expert_in: bfloat16 [8, 384, 1536], P('expert'), may hold values from -0.3125 to 0.3125
- expert_out: bfloat16 [8, 1536, 384], P('expert'), may hold values from -2.5 to 2.5
- master_in: float32 [8, 384, 1536], P('expert', 'dp'), may hold values from -0.3125 to 0.3125
- master_out: float32 [8, 1536, 384], P('expert', 'dp'), may hold values from -0.15625 to 0.15625
- moment_in: float32 [8, 384, 1536], P('expert', 'dp'), may hold values from -6 to 6
- moment_out: float32 [8, 1536, 384], P('expert', 'dp'), may hold values from -6 to 6
- second_in: float32 [8, 384, 1536], P('expert', 'dp'), may hold values from 0.01 to 1
- second_out: float32 [8, 1536, 384], P('expert', 'dp'), may hold values from 0.01 to 1
Outputs:
- block_out: bfloat16 [256, 197, 384], P(('dp', 'expert'))
- images_grad: bfloat16 [256, 197, 384], P(('dp', 'expert'))
- norm1_gain_grad: float32 [384], replicated
- norm1_shift_grad: float32 [384], replicated
- query_weight_grad: float32 [384, 384], replicated
- query_bias_grad: float32 [384], replicated
- key_weight_grad: float32 [384, 384], replicated
- value_weight_grad: float32 [384, 384], replicated
- value_bias_grad: float32 [384], replicated
- output_weight_grad: float32 [384, 384], replicated
- output_bias_grad: float32 [384], replicated
- norm2_gain_grad: float32 [384], replicated
- norm2_shift_grad: float32 [384], replicated
- router_weight_grad: float32 [384, 8], replicated
- new_expert_in: bfloat16 [8, 384, 1536], P('expert')
- new_expert_out: bfloat16 [8, 1536, 384], P('expert')
- new_master_in: float32 [8, 384, 1536], P('expert', 'dp')
- new_master_out: float32 [8, 1536, 384], P('expert', 'dp')
- new_moment_in: float32 [8, 384, 1536], P('expert', 'dp')
- new_moment_out: float32 [8, 1536, 384], P('expert', 'dp')
- new_second_in: float32 [8, 384, 1536], P('expert', 'dp')
- new_second_out: float32 [8, 1536, 384], P('expert', 'dp')
Inputs may be any that keep to these rules, and one draw needn't show every extreme that they name: `routes`: each token names 2 different experts. `seat_order`: each row holds every number of 0 to 3151 once.
All inputs are finite; a program needn't handle non-finite values.
Results may differ from a plain program's by a relative error of at most 0.02.
Values may be sent and summed in bfloat16 or wider, within the bound.
No kernel may reach another device: no remote copies, remote signals or barrier semaphores. Data moves between devices by JAX's collectives and lax.ppermute only.
A program may use at most 256 MiB of HBM per device.

v0:
```python
import jax
import jax.numpy as jnp
from jax import lax
from jax.sharding import PartitionSpec as P

HEADS = 6


EPS_NORM = 1e-06
BETA_ONE = 0.9
BETA_TWO = 0.999
LEARN_RATE = 0.03
ADAM_EPS = 1e-08
adam_steps = 100.0


def softmax_rows(values):
    peak = jnp.max(values, axis=-1, keepdims=True)
    expo = jnp.exp(values - peak)
    return expo / jnp.sum(expo, axis=-1, keepdims=True)


def norm_forward(values, gain, shift):
    mean = jnp.mean(values, axis=-1, keepdims=True)
    centred = values - mean
    inverse = lax.rsqrt(jnp.mean(centred * centred, axis=-1, keepdims=True) + EPS_NORM)
    unit = centred * inverse
    return (unit * gain + shift, unit, inverse)


def norm_backward(grad, unit, inverse, gain):
    scaled = grad * gain
    inner = (
        scaled
        - jnp.mean(scaled, axis=-1, keepdims=True)
        - unit * jnp.mean(scaled * unit, axis=-1, keepdims=True)
    )
    return (inverse * inner, jnp.sum(grad * unit, axis=0), jnp.sum(grad, axis=0))


def contract_rows(left, right):
    return lax.dot_general(
        left, right, (((0,), (0,)), ((), ())), preferred_element_type=jnp.float32
    )


def contract_cols(left, right):
    return lax.dot_general(
        left, right, (((1,), (1,)), ((), ())), preferred_element_type=jnp.float32
    )


def gelu_plain(values):
    return jax.nn.gelu(values, approximate=True)


def gelu_grad(pre_act, grad):
    _, pullback = jax.vjp(gelu_plain, pre_act)
    return pullback(grad)[0]


def adam_step(master, moment, second, grad):
    new_moment = BETA_ONE * moment + (1.0 - BETA_ONE) * grad
    new_second = BETA_TWO * second + (1.0 - BETA_TWO) * grad * grad
    corr_one = 1.0 - BETA_ONE**adam_steps
    corr_two = 1.0 - BETA_TWO**adam_steps
    update = LEARN_RATE * (new_moment / corr_one) / (jnp.sqrt(new_second / corr_two) + ADAM_EPS)
    return (master - update, new_moment, new_second)


def on_device(
    images,
    cotangent,
    router_noise,
    routes,
    seat_order,
    norm1_gain,
    norm1_shift,
    query_weight,
    query_bias,
    key_weight,
    value_weight,
    value_bias,
    output_weight,
    output_bias,
    norm2_gain,
    norm2_shift,
    router_weight,
    expert_in,
    expert_out,
    master_in,
    master_out,
    moment_in,
    moment_out,
    second_in,
    second_out,
):
    lowp = jnp.bfloat16
    wide = jnp.float32
    img_count, seq_len, width = images.shape
    tokens = img_count * seq_len
    experts = router_noise.shape[2]
    top_count = routes.shape[2]
    pair_count = tokens * top_count
    capacity = (pair_count + experts - 1) // experts
    slot_count = experts * capacity
    head_count = HEADS
    head_size = width // head_count
    score_scale = head_size ** (-0.5)
    inner_width = expert_in.shape[2]
    weight_in = expert_in[0]
    weight_out = expert_out[0]
    route_flat = routes.reshape(pair_count)
    order_flat = seat_order.reshape(pair_count)
    expert_ids = lax.broadcasted_iota(jnp.int32, (pair_count, experts), 1)
    chosen = route_flat[:, None] == expert_ids
    earlier = (order_flat[None, :] < order_flat[:, None]).astype(lowp)
    counts = jnp.dot(earlier, chosen.astype(lowp), preferred_element_type=wide)
    position = jnp.sum(jnp.where(chosen, counts, 0.0), axis=1).astype(jnp.int32)
    seated = position < capacity
    slot_of = route_flat * capacity + position
    slot_ids = lax.broadcasted_iota(jnp.int32, (pair_count, slot_count), 1)
    pair_hits = ((slot_of[:, None] == slot_ids) & seated[:, None]).reshape(
        tokens, top_count, slot_count
    )
    dispatch = jnp.any(pair_hits, axis=1).astype(lowp)
    seated_pairs = seated.reshape(tokens, top_count).astype(wide)
    route_hot = routes.reshape(tokens, top_count)[:, :, None] == lax.broadcasted_iota(
        jnp.int32, (tokens, top_count, experts), 2
    )
    x_rows = images.reshape(tokens, width).astype(wide)
    normed, unit_one, inverse_one = norm_forward(x_rows, norm1_gain, norm1_shift)
    normed_b = normed.astype(lowp)
    query_rows = (jnp.dot(normed_b, query_weight, preferred_element_type=wide) + query_bias).astype(
        lowp
    )
    key_rows = jnp.dot(normed_b, key_weight, preferred_element_type=wide).astype(lowp)
    value_rows = (jnp.dot(normed_b, value_weight, preferred_element_type=wide) + value_bias).astype(
        lowp
    )
    split = (img_count, seq_len, head_count, head_size)
    query4 = query_rows.reshape(split)
    key4 = key_rows.reshape(split)
    value4 = value_rows.reshape(split)
    scores = jnp.einsum("ishd,ithd->ihst", query4, key4, preferred_element_type=wide) * score_scale
    peak = jnp.max(scores, axis=-1, keepdims=True)
    expo = jnp.exp(scores - peak)
    total = jnp.sum(expo, axis=-1, keepdims=True)
    log_total = peak + jnp.log(total)
    attention_b = (expo / total).astype(lowp)
    mixed_rows = (
        jnp.einsum("ihst,ithd->ishd", attention_b, value4, preferred_element_type=wide)
        .reshape(tokens, width)
        .astype(lowp)
    )
    state = x_rows + jnp.dot(mixed_rows, output_weight, preferred_element_type=wide) + output_bias
    routed, unit_two, inverse_two = norm_forward(state, norm2_gain, norm2_shift)
    routed_b = routed.astype(lowp)
    logits = jnp.dot(routed_b, router_weight, preferred_element_type=wide) + router_noise.reshape(
        tokens, experts
    )
    gate_probs = softmax_rows(logits)
    gate_pair = jnp.sum(jnp.where(route_hot, gate_probs[:, None, :], 0.0), axis=2)
    gates = (gate_pair * seated_pairs).astype(lowp)
    combine = jnp.sum(jnp.where(pair_hits, gates.astype(wide)[:, :, None], 0.0), axis=1).astype(
        lowp
    )
    sent = (
        jnp.einsum("ts,td->sd", dispatch, routed_b, preferred_element_type=wide)
        .astype(lowp)
        .reshape(experts, capacity, width)
    )
    arrived_rows = lax.all_to_all(sent, "expert", split_axis=0, concat_axis=0, tiled=True)
    sources, items, _ = arrived_rows.shape
    flat = arrived_rows.reshape(sources * items, width)
    pre_act = jnp.dot(flat, weight_in, preferred_element_type=wide)
    activated = gelu_plain(pre_act).astype(lowp)
    produced = jnp.dot(activated, weight_out, preferred_element_type=wide).astype(lowp)
    returned_rows = lax.all_to_all(
        produced.reshape(sources, items, width), "expert", split_axis=0, concat_axis=0, tiled=True
    )
    results = (
        returned_rows,
        arrived_rows,
        activated.reshape(sources, items, inner_width),
        pre_act.reshape(sources, items, inner_width),
    )
    returned = results[0].reshape(slot_count, width)
    arrived = results[1].reshape(slot_count, width)
    block_rows = state + jnp.dot(combine, returned, preferred_element_type=wide)
    block_out = block_rows.astype(lowp).reshape(images.shape)
    grad_rows = cotangent.reshape(tokens, width)
    grad_wide = grad_rows.astype(wide)
    slot_grad = (
        jnp.einsum("ts,td->sd", combine, grad_rows, preferred_element_type=wide)
        .astype(lowp)
        .reshape(experts, capacity, width)
    )
    arrived_grad = lax.all_to_all(
        slot_grad, "expert", split_axis=0, concat_axis=0, tiled=True
    ).reshape(slot_count, width)
    activated = results[2].reshape(slot_count, inner_width)
    pre_act = results[3].reshape(slot_count, inner_width)
    hidden_grad = contract_cols(arrived_grad, weight_out)
    grad_weight_out = contract_rows(activated, arrived_grad)
    pre_grad = gelu_grad(pre_act, hidden_grad).astype(lowp)
    grad_weight_in = contract_rows(arrived, pre_grad)
    row_grad = contract_cols(pre_grad, weight_in).astype(lowp).reshape(experts, capacity, width)
    token_grad = lax.all_to_all(
        row_grad, "expert", split_axis=0, concat_axis=0, tiled=True
    ).reshape(slot_count, width)
    pair_rows = jnp.einsum(
        "tks,sd->tkd", pair_hits.astype(lowp), returned, preferred_element_type=wide
    )
    gate_grad = jnp.sum(pair_rows * grad_wide[:, None, :], axis=2) * seated_pairs
    prob_grad = jnp.sum(jnp.where(route_hot, gate_grad[:, :, None], 0.0), axis=1)
    logit_grad = (
        gate_probs * (prob_grad - jnp.sum(gate_probs * prob_grad, axis=1, keepdims=True))
    ).astype(lowp)
    router_grad = contract_rows(logit_grad, routed_b)
    routed_grad = jnp.dot(dispatch, token_grad, preferred_element_type=wide) + contract_cols(
        logit_grad, router_weight
    )
    state_part, gain_two_grad, shift_two_grad = norm_backward(
        routed_grad, unit_two, inverse_two, norm2_gain
    )
    state_grad = grad_wide + state_part
    branch_grad = state_grad.astype(lowp)
    out_bias_grad = jnp.sum(branch_grad.astype(wide), axis=0)
    out_weight_grad = contract_rows(mixed_rows, branch_grad)
    mixed_grad = contract_cols(branch_grad, output_weight).astype(lowp).reshape(split)
    scores_again = (
        jnp.einsum("ishd,ithd->ihst", query4, key4, preferred_element_type=wide) * score_scale
    )
    probs_again = jnp.exp(scores_again - log_total)
    weights_again = probs_again.astype(lowp)
    weight_grad = jnp.einsum("ishd,ithd->ihst", mixed_grad, value4, preferred_element_type=wide)
    value_grad = (
        jnp.einsum("ihst,ishd->ithd", weights_again, mixed_grad, preferred_element_type=wide)
        .astype(lowp)
        .reshape(tokens, width)
    )
    score_grad = (
        probs_again * (weight_grad - jnp.sum(probs_again * weight_grad, axis=-1, keepdims=True))
    ).astype(lowp)
    query_grad = (
        (jnp.einsum("ihst,ithd->ishd", score_grad, key4, preferred_element_type=wide) * score_scale)
        .astype(lowp)
        .reshape(tokens, width)
    )
    key_grad = (
        (
            jnp.einsum("ihst,ishd->ithd", score_grad, query4, preferred_element_type=wide)
            * score_scale
        )
        .astype(lowp)
        .reshape(tokens, width)
    )
    query_weight_part = contract_rows(normed_b, query_grad)
    key_weight_part = contract_rows(normed_b, key_grad)
    value_weight_part = contract_rows(normed_b, value_grad)
    query_bias_part = jnp.sum(query_grad.astype(wide), axis=0)
    value_bias_part = jnp.sum(value_grad.astype(wide), axis=0)
    normed_grad = (
        contract_cols(query_grad, query_weight)
        + contract_cols(key_grad, key_weight)
        + contract_cols(value_grad, value_weight)
    )
    x_part, gain_one_grad, shift_one_grad = norm_backward(
        normed_grad, unit_one, inverse_one, norm1_gain
    )
    images_grad = (state_grad + x_part).astype(lowp).reshape(images.shape)
    weight_stack = jnp.stack(
        [query_weight_part, key_weight_part, value_weight_part, out_weight_grad]
    )
    small_stack = jnp.concatenate(
        [
            jnp.stack(
                [
                    query_bias_part,
                    value_bias_part,
                    out_bias_grad,
                    gain_one_grad,
                    shift_one_grad,
                    gain_two_grad,
                    shift_two_grad,
                ]
            ),
            router_grad,
        ],
        axis=0,
    )
    weight_sum, small_sum = lax.psum((weight_stack, small_stack), ("dp", "expert"))
    share_in, share_out = (
        lax.psum_scatter(
            grad_weight_in[None].astype(jnp.bfloat16), "dp", scatter_dimension=1, tiled=True
        ).astype(jnp.float32),
        lax.psum_scatter(
            grad_weight_out[None].astype(jnp.bfloat16), "dp", scatter_dimension=1, tiled=True
        ).astype(jnp.float32),
    )
    new_master_in, new_moment_in, new_second_in = adam_step(
        master_in, moment_in, second_in, share_in
    )
    new_master_out, new_moment_out, new_second_out = adam_step(
        master_out, moment_out, second_out, share_out
    )
    new_expert_in, new_expert_out = (
        lax.all_gather(new_master_in.astype(lowp), "dp", axis=1, tiled=True),
        lax.all_gather(new_master_out.astype(lowp), "dp", axis=1, tiled=True),
    )
    return (
        block_out,
        images_grad,
        small_sum[3],
        small_sum[4],
        weight_sum[0],
        small_sum[0],
        weight_sum[1],
        weight_sum[2],
        small_sum[1],
        weight_sum[3],
        small_sum[2],
        small_sum[5],
        small_sum[6],
        small_sum[7:].T,
        new_expert_in,
        new_expert_out,
        new_master_in,
        new_master_out,
        new_moment_in,
        new_moment_out,
        new_second_in,
        new_second_out,
    )


def solution(mesh):
    in_specs = (
        P(("dp", "expert"), None, None),
        P(("dp", "expert"), None, None),
        P(("dp", "expert"), None, None),
        P(("dp", "expert"), None, None),
        P(("dp", "expert"), None),
        P(),
        P(),
        P(),
        P(),
        P(),
        P(),
        P(),
        P(),
        P(),
        P(),
        P(),
        P(),
        P("expert", None, None),
        P("expert", None, None),
        P("expert", "dp", None),
        P("expert", "dp", None),
        P("expert", "dp", None),
        P("expert", "dp", None),
        P("expert", "dp", None),
        P("expert", "dp", None),
    )
    out_specs = (
        P(("dp", "expert"), None, None),
        P(("dp", "expert"), None, None),
        P(),
        P(),
        P(),
        P(),
        P(),
        P(),
        P(),
        P(),
        P(),
        P(),
        P(),
        P(),
        P("expert", None, None),
        P("expert", None, None),
        P("expert", "dp", None),
        P("expert", "dp", None),
        P("expert", "dp", None),
        P("expert", "dp", None),
        P("expert", "dp", None),
        P("expert", "dp", None),
    )
    return jax.shard_map(
        on_device, mesh=mesh, in_specs=in_specs, out_specs=out_specs, check_vma=False
    )
```

profile of v0, /device:TPU:0, one launch (start us, length us, event | category | flops | bytes accessed | tf_op | source)
XLA Modules:
  0.0 636.4 jit_solution(13968139022859609547)
XLA Ops:
  14.9 6.1 fusion.60
  31.0 5.2 reshape.353
  79.6 15.1 %fusion.1 = pred[1576,3152]{1,0:T(8,128)(4,1)S(1)} fusion(s32[1576,2]{0,1:T(2,128)S(1)} %multiply_add_fusion.1, pred[1576,2]{0,1:T(4,128)(4,1)S(1)} %broadcast_compare_fusion), kind=kLoop, calls=%fused_computation.4 | loop fusion | flops 24837760 | bytes 4983312 | tf_op jit(solution)/shard_map/reduce_or | solution.py:126
  96.9 12.6 %convolution_convert_fusion.3 = bf16[3152,384]{1,0:T(8,128)(2,1)} fusion(pred[1576,3152]{1,0:T(8,128)(4,1)S(1)} %fusion.1, bf16[1576,384]{1,0:T(8,128)(2,1)S(1)} %add_convert_fusion.2), kind=kOutput, calls=%fused_computation.35 | convolution fusion | flops 3816290304 | bytes 8598656 | tf_op jit(solution)/shard_map/ts,td->sd/dot_general | solution.py:169
  112.8 35.7 %all_to_all.20 = bf16[8,394,384]{2,1,0:T(8,128)(2,1)} all-to-all(bf16[8,394,384]{2,1,0:T(8,128)(2,1)} %reshape.335), channel_id=1, replica_groups=mesh['dp'=4,'expert'=8] {'expert'}, dimensions={0} | all-to-all | bytes 4841472 | tf_op jit(solution)/shard_map/all_to_all | solution.py:173
  151.5 13.9 %multiply_convert_fusion = (bf16[3152,1536]{1,0:T(8,128)(2,1)S(1)}, f32[3152,1536]{1,0:T(8,128)}) fusion(bf16[3152,384]{1,0:T(8,128)(2,1)} %reshape.336, bf16[1,384,1536]{2,1,0:T(8,128)(2,1)S(1)} %copy-done), kind=kOutput, calls=%fused_computation.23 | convolution fusion | flops 3761823744 | bytes 32649216 | tf_op jit(solution)/shard_map/dot_general | solution.py:176
  169.1 6.5 %convolution_convert_fusion.2 = bf16[3152,384]{1,0:T(8,128)(2,1)} fusion(bf16[3152,1536]{1,0:T(8,128)(2,1)S(1)} %get-tuple-element.167, bf16[1,1536,384]{2,1,0:T(8,128)(2,1)S(1)} %copy-done.68), kind=kOutput, calls=%fused_computation.34 | convolution fusion | flops 3719460864 | bytes 13283328 | tf_op jit(solution)/shard_map/dot_general | solution.py:178
  191.9 21.8 %all-to-all-done.1 = bf16[8,394,384]{2,1,0:T(8,128)(2,1)} async-done(((bf16[8,394,384]{2,1,0:T(8,128)(2,1)}), bf16[8,394,384]{2,1,0:T(8,128)(2,1)}, u32[]{:S(2)}, u32[]{:S(2)}) %all-to-all-start.1) | async-done | bytes 2420768 | tf_op jit(solution)/shard_map/all_to_all | solution.py:179
  217.1 15.0 %multiply_reduce_fusion.2 = f32[1576,2]{0,1:T(2,128)S(1)} fusion(bf16[3152,384,1]{1,0,2:T(8,128)(2,1)} %reshape.351, s32[1576,2]{0,1:T(2,128)S(1)} %multiply_add_fusion.1, pred[1576,2]{0,1:T(4,128)(4,1)S(1)} %broadcast_compare_fusion, f32[1576,384]{1,0:T(8,128)} %convert_element_type.210), kind=kOutput, calls=%fused_computation.43 | convolution fusion | flops 7652447744 | bytes 4869840 | tf_op jit(solution)/shard_map/tks,sd->tkd/dot_general | solution.py:212
  232.2 19.7 %select_reduce_fusion = bf16[1576,3152]{1,0:T(8,128)(2,1)S(1)} fusion(f32[1576,2]{0,1:T(2,128)S(1)} %fusion.70, s32[1576,2]{0,1:T(2,128)S(1)} %multiply_add_fusion.1, pred[1576,2]{0,1:T(4,128)(4,1)S(1)} %broadcast_compare_fusion), kind=kLoop, calls=%fused_computation.1 | loop fusion | flops 34772864 | bytes 9963472 | tf_op jit(solution)/shard_map/reduce_sum | solution.py:165
  255.7 7.4 %convolution_convert_fusion.1 = bf16[3152,384]{1,0:T(8,128)(2,1)} fusion(bf16[1576,384]{1,0:T(8,128)(2,1)S(1)} %copy-done.16, bf16[1576,3152]{1,0:T(8,128)(2,1)S(1)} %select_reduce_fusion), kind=kOutput, calls=%fused_computation.33 | convolution fusion | flops 3816290304 | bytes 13566208 | tf_op jit(solution)/shard_map/ts,td->sd/dot_general | solution.py:195
  266.2 35.1 %all_to_all.21 = bf16[8,394,384]{2,1,0:T(8,128)(2,1)} all-to-all(bf16[8,394,384]{2,1,0:T(8,128)(2,1)} %reshape.341), channel_id=1, replica_groups=mesh['dp'=4,'expert'=8] {'expert'}, dimensions={0} | all-to-all | bytes 4841472 | tf_op jit(solution)/shard_map/all_to_all | solution.py:199
  304.3 9.7 %fusion.43 = bf16[1,1536,384]{2,1,0:T(8,128)(2,1)} fusion(bf16[3152,1536]{1,0:T(8,128)(2,1)} %copy-done.72, bf16[3152,384]{1,0:T(8,128)(2,1)} %reshape.342), kind=kOutput, calls=%fused_computation.64 | convolution fusion | flops 3718840320 | bytes 13283328 | tf_op jit(solution)/shard_map/dot_general | solution.py:42
  314.0 22.3 %fusion.18 = bf16[3152,1536]{1,0:T(8,128)(2,1)} fusion(f32[3152,1536]{1,0:T(8,128)} %get-tuple-element.168, bf16[3152,384]{1,0:T(8,128)(2,1)} %reshape.342, bf16[1,1536,384]{2,1,0:T(8,128)(2,1)S(1)} %copy-done.69), kind=kOutput, calls=%fused_computation.22 | convolution fusion | flops 3815079936 | bytes 32649216 | tf_op jit(solution)/shard_map/dot_general | solution.py:48
  336.3 10.2 %convolution_convert_fusion = bf16[3152,384]{1,0:T(8,128)(2,1)} fusion(bf16[3152,1536]{1,0:T(8,128)(2,1)} %fusion.18, bf16[1,384,1536]{2,1,0:T(8,128)(2,1)S(1)} %copy-done), kind=kOutput, calls=%fused_computation.32 | convolution fusion | flops 3719460864 | bytes 13283328 | tf_op jit(solution)/shard_map/dot_general | solution.py:48
  360.1 9.7 %fusion.44 = bf16[1,384,1536]{2,1,0:T(8,128)(2,1)} fusion(bf16[3152,384]{1,0:T(8,128)(2,1)} %reshape.336, bf16[3152,1536]{1,0:T(8,128)(2,1)} %fusion.18), kind=kOutput, calls=%fused_computation.65 | convolution fusion | flops 3718840320 | bytes 13283328 | tf_op jit(solution)/shard_map/dot_general | solution.py:42
  369.9 14.8 %all-to-all-done.3 = bf16[8,394,384]{2,1,0:T(8,128)(2,1)} async-done(((bf16[8,394,384]{2,1,0:T(8,128)(2,1)}), bf16[8,394,384]{2,1,0:T(8,128)(2,1)}, u32[]{:S(2)}, u32[]{:S(2)}) %all-to-all-start.3) | async-done | bytes 2420768 | tf_op jit(solution)/shard_map/all_to_all | solution.py:209
  387.7 8.5 %fusion.83 = f32[1576,384]{1,0:T(8,128)S(1)} fusion(pred[1576,3152]{1,0:T(8,128)(4,1)} %copy-done.25, bf16[3152,384]{1,0:T(8,128)(2,1)} %reshape.344), kind=kOutput, calls=%fused_computation.155 | convolution fusion | flops 3815079936 | bytes 9809024 | tf_op jit(solution)/shard_map/dot_general | solution.py:221
  408.7 8.8 %multiply_reduce_fusion = (f32[8,6,197]{2,1,0:T(8,128)S(1)}, f32[8,6,197,197]{2,3,1,0:T(8,128)}) fusion(f32[8,6,197,197]{2,3,1,0:T(8,128)} %copy-done.1, f32[8,6,197]{2,1,0:T(8,128)S(1)} %log_add_fusion, bf16[8,197,6,64]{1,3,2,0:T(8,128)(2,1)S(1)} %copy.197, bf16[8,197,6,64]{1,3,2,0:T(8,128)(2,1)} %copy.187), kind=kOutput, calls=%fused_computation.25 | convolution fusion | flops 245884368 | bytes 17399040 | tf_op jit(solution)/shard_map/ishd,ithd->ihst/dot_general | solution.py:237
  417.5 11.5 %multiply_convert_fusion.1 = bf16[8,6,197,197]{2,3,1,0:T(8,128)(2,1)} fusion(f32[8,6,197,197]{2,3,1,0:T(8,128)} %get-tuple-element.173, f32[8,6,197,197]{2,3,1,0:T(8,128)} %copy-done.1, f32[8,6,197]{2,1,0:T(8,128)S(1)} %get-tuple-element.172, f32[8,6,197]{2,1,0:T(8,128)S(1)} %log_add_fusion), kind=kLoop, calls=%fused_computation.24 | loop fusion | flops 9314160 | bytes 18703968 | tf_op jit(solution)/shard_map/convert_element_type | solution.py:245
  429.0 5.9 convert_reduce_fusion
  467.1 10.2 %fusion.40 = bf16[1576,384]{1,0:T(8,128)(2,1)} fusion(f32[1576,384]{1,0:T(8,128)} %copy-done.2, bf16[3152,384]{1,0:T(8,128)(2,1)} %reshape.338, bf16[1576,3152]{1,0:T(8,128)(2,1)} %copy-done.18), kind=kOutput, calls=%fused_computation.63 | convolution fusion | flops 3816290304 | bytes 15986944 | tf_op jit(solution)/shard_map/dot_general | solution.py:190
  503.4 41.5 %psum.14 = f32[15,384]{1,0:T(8,128)S(1)} all-reduce(f32[15,384]{1,0:T(8,128)S(1)} %concatenate.3), channel_id=1, replica_groups=mesh['dp'=4,'expert'=8] {'dp','expert'}, use_global_device_ids=true, to_apply=%region_27.28 | all-reduce | flops 5760 | bytes 46080 | tf_op jit(solution)/shard_map/psum | solution.py:293
  546.1 76.2 %all-reduce.2.cloned.1.call-done = f32[4,384,384]{2,1,0:T(8,128)} async-done(((f32[4,384,384]{2,1,0:T(8,128)}), f32[4,384,384]{2,1,0:T(8,128)}) %all-reduce.2.cloned.1.call-update) | async-done | bytes 2359312 | tf_op jit(solution)/shard_map/psum | solution.py:293
  (274 shorter events, 196.2 us)
Async XLA Ops:
  8.0 143.5 %copy-start = (bf16[1,384,1536]{2,1,0:T(8,128)(2,1)S(1)}, bf16[1,384,1536]{2,1,0:T(8,128)(2,1)}, u32[]{:S(2)}) copy-start(bf16[1,384,1536]{2,1,0:T(8,128)(2,1)} %param.42) | copy-start | bytes 3538948
  9.9 15.7 %copy-start.51 = (f32[1576]{0:T(1024)}, f32[1576]{0:T(1024)S(1)}, u32[]{:S(2)}) copy-start(f32[1576]{0:T(1024)S(1)} %div.65) | copy-start | bytes 18916
  14.4 6.6 %copy-start.55 = (f32[8,197]{1,0:T(8,128)}, f32[8,197]{1,0:T(8,128)S(1)}, u32[]{:S(2)}) copy-start(f32[8,197]{1,0:T(8,128)S(1)} %add_rsqrt_fusion.1) | copy-start | bytes 18916
  14.5 11.1 %copy-start.53 = (f32[1576]{0:T(1024)}, f32[1576]{0:T(1024)S(1)}, u32[]{:S(2)}) copy-start(f32[1576]{0:T(1024)S(1)} %rsqrt.21) | copy-start | bytes 18916
  78.9 15.8 %copy-start.2 = (f32[1576,384]{1,0:T(8,128)}, f32[1576,384]{1,0:T(8,128)S(1)}, u32[]{:S(2)}) copy-start(f32[1576,384]{1,0:T(8,128)S(1)} %get-tuple-element.166) | copy-start | bytes 7262212
  78.9 15.7 %copy-start.47 = (f32[1576]{0:T(1024)}, f32[1576]{0:T(1024)S(1)}, u32[]{:S(2)}) copy-start(f32[1576]{0:T(1024)S(1)} %broadcast_multiply_fusion.4) | copy-start | bytes 18916
  79.5 15.2 %copy-start.49 = (f32[1576]{0:T(1024)}, f32[1576]{0:T(1024)S(1)}, u32[]{:S(2)}) copy-start(f32[1576]{0:T(1024)S(1)} %add_rsqrt_fusion) | copy-start | bytes 18916
  79.5 15.2 %copy-start.61 = (f32[384]{0:T(512)S(1)}, f32[384]{0:T(512)}, u32[]{:S(2)}) copy-start(f32[384]{0:T(512)} %param.39) | copy-start | bytes 4612
  79.5 15.2 %copy-start.67 = (f32[384]{0:T(512)S(1)}, f32[384]{0:T(512)}, u32[]{:S(2)}) copy-start(f32[384]{0:T(512)} %param.40) | copy-start | bytes 4612
  96.9 94.5 %copy-start.14 = (bf16[1576,384]{1,0:T(8,128)(2,1)}, bf16[1576,384]{1,0:T(8,128)(2,1)S(1)}, u32[]{:S(2)}) copy-start(bf16[1576,384]{1,0:T(8,128)(2,1)S(1)} %add_convert_fusion.2) | copy-start | bytes 3631108
  151.5 17.6 %copy-start.68 = (bf16[1,1536,384]{2,1,0:T(8,128)(2,1)S(1)}, bf16[1,1536,384]{2,1,0:T(8,128)(2,1)}, u32[]{:S(2)}) copy-start(bf16[1,1536,384]{2,1,0:T(8,128)(2,1)} %param.43) | copy-start | bytes 3538948
  178.6 35.1 %all-to-all-start.1 = ((bf16[8,394,384]{2,1,0:T(8,128)(2,1)}), bf16[8,394,384]{2,1,0:T(8,128)(2,1)}, u32[]{:S(2)}, u32[]{:S(2)}) async-start(bf16[8,394,384]{2,1,0:T(8,128)(2,1)} %reshape.337), calls=%async_computation.1 | async-start | bytes 4915200 | tf_op jit(solution)/shard_map/all_to_all | solution.py:179
  183.2 300.0 %reduce-scatter.5.cloned.1.call-start = ((), (), s32[]{:S(2)}) async-start(), calls=%async_computation.9 | async-start | bytes 1474560 | tf_op jit(solution)/shard_map/reduce_scatter | solution.py:298
  232.2 23.5 %copy-start.16 = (bf16[1576,384]{1,0:T(8,128)(2,1)S(1)}, bf16[1576,384]{1,0:T(8,128)(2,1)}, u32[]{:S(2)}) copy-start(bf16[1576,384]{1,0:T(8,128)(2,1)} %reshape.340) | copy-start | bytes 3631108
  304.3 9.7 %copy-start.69 = (bf16[1,1536,384]{2,1,0:T(8,128)(2,1)S(1)}, bf16[1,1536,384]{2,1,0:T(8,128)(2,1)}, u32[]{:S(2)}) copy-start(bf16[1,1536,384]{2,1,0:T(8,128)(2,1)} %param.43) | copy-start | bytes 3538948
  349.6 35.0 %all-to-all-start.3 = ((bf16[8,394,384]{2,1,0:T(8,128)(2,1)}), bf16[8,394,384]{2,1,0:T(8,128)(2,1)}, u32[]{:S(2)}, u32[]{:S(2)}) async-start(bf16[8,394,384]{2,1,0:T(8,128)(2,1)} %reshape.343), calls=%async_computation.3 | async-start | bytes 4915200 | tf_op jit(solution)/shard_map/all_to_all | solution.py:209
  354.1 139.1 %reduce-scatter.3.cloned.1.call-start = ((), (), s32[]{:S(2)}) async-start(), calls=%async_computation.7 | async-start | bytes 1474560 | tf_op jit(solution)/shard_map/reduce_scatter | solution.py:295
  369.8 252.4 %all-reduce.2.cloned.1.call-start = ((), (), s32[]{:S(2)}) async-start(), calls=%async_computation.6 | async-start | bytes 4718592 | tf_op jit(solution)/shard_map/psum | solution.py:293
  387.7 8.5 %copy-start.3 = (f32[1576,384]{1,0:T(8,128)S(1)}, f32[1576,384]{1,0:T(8,128)}, u32[]{:S(2)}) copy-start(f32[1576,384]{1,0:T(8,128)} %copy-done.2) | copy-start | bytes 7262212
  387.7 8.5 %copy-start.48 = (f32[1576]{0:T(1024)S(1)}, f32[1576]{0:T(1024)}, u32[]{:S(2)}) copy-start(f32[1576]{0:T(1024)} %copy-done.47) | copy-start | bytes 18916
  387.7 8.5 %copy-start.50 = (f32[1576]{0:T(1024)S(1)}, f32[1576]{0:T(1024)}, u32[]{:S(2)}) copy-start(f32[1576]{0:T(1024)} %copy-done.49) | copy-start | bytes 18916
  387.7 8.5 %copy-start.62 = (f32[384]{0:T(512)S(1)}, f32[384]{0:T(512)}, u32[]{:S(2)}) copy-start(f32[384]{0:T(512)} %param.39) | copy-start | bytes 4612
  467.0 158.2 %all-gather.5.cloned.1.call-start = ((), (), s32[]{:S(2)}) async-start(), calls=%async_computation.10 | async-start | bytes 1474560 | tf_op jit(solution)/shard_map/all_gather | solution.py:310
  486.2 139.1 %all-gather.3.cloned.1.call-start = ((), (), s32[]{:S(2)}) async-start(), calls=%async_computation.8 | async-start | bytes 1474560 | tf_op jit(solution)/shard_map/all_gather | solution.py:309
  (56 other events, 182.0 us)
Sparse Core Ops, SparseCore 0:
  336.4 29.1 reduce-scatter.4
  369.9 31.3 reduce-scatter.2
  486.3 31.7 all-gather.4
  520.2 30.9 all-gather.2
Sparse Core Ops, SparseCore 1:
  467.1 155.1 all-reduce.1
where the time goes:
time: 647 us; the launch traced here: 636 us
  matrix products  185 us (29%)
  local copies, waits for them, and re-layouts  130 us (20%)
  waiting for transfers between devices  113 us (17%)
  blocking collectives  112 us (17%)
  other arithmetic  70.8 us (11%)
  between operations  16.8 us (3%)
  starting transfers between devices  9.51 us (1%)
    psum x1, waiting for transfers between devices, on_device(): lax.psum((weight_stack, small_stack), ('dp', 'expert'))  76.2 us
    psum x1, blocking collectives, on_device(): lax.psum((weight_stack, small_stack), ('dp', 'expert'))  41.5 us
    dot_general x7, matrix products, contract_cols(): lax.dot_general(left, right, (((1,), (1,)), ((), ())), preferred_element_...  40.9 us
    all_to_all x1, blocking collectives, on_device(): lax.all_to_all(sent, 'expert', split_axis=0, concat_axis=0, tiled=True)  35.7 us
    all_to_all x1, blocking collectives, on_device(): lax.all_to_all(slot_grad, 'expert', split_axis=0, concat_axis=0, tiled=True)  35.1 us
    unnamed x154, local copies, waits for them, and re-layouts  26.8 us
    dot_general x7, matrix products, contract_rows(): lax.dot_general(left, right, (((0,), (0,)), ((), ())), preferred_element_...  25.2 us
    all_to_all x1, waiting for transfers between devices, on_device(): lax.all_to_all(produced.reshape(sources, items, width), 'expert', split_a...  21.8 us
  transfers between devices with their start and end apart: 7, of which 3 were waited for; matrix products, arithmetic and copies ran while one was open for 24% of the time, Pallas kernels for 0%

commit v1 on v0

v1 whole, which is shorter than its diff:
```python
import functools

import jax
import jax.numpy as jnp
from jax import lax
from jax.experimental import pallas as pl
from jax.experimental.pallas import tpu as pltpu
from jax.sharding import PartitionSpec as P

HEADS = 6
EPS_NORM = 1e-06
BETA_ONE = 0.9
BETA_TWO = 0.999
LEARN_RATE = 0.03
ADAM_EPS = 1e-08
adam_steps = 100.0

lowp = jnp.bfloat16
wide = jnp.float32
LANES = 128
HALF = 64
VMEM_BYTES = 56 * 1024 * 1024


def round_up(value, step):
    return (value + step - 1) // step * step


def dot(left, right):
    return jnp.dot(left, right, preferred_element_type=wide)


def dot_nt(left, right):
    return lax.dot_general(left, right, (((1,), (1,)), ((), ())), preferred_element_type=wide)


def dot_tn(left, right):
    return lax.dot_general(left, right, (((0,), (0,)), ((), ())), preferred_element_type=wide)


def iota(shape, dim):
    return lax.broadcasted_iota(jnp.int32, shape, dim)


def params(dims):
    return pltpu.CompilerParams(
        dimension_semantics=("arbitrary",) * dims, vmem_limit_bytes=VMEM_BYTES
    )


def unit_norm(values):
    mean = jnp.mean(values, axis=-1, keepdims=True)
    centred = values - mean
    inverse = lax.rsqrt(jnp.mean(centred * centred, axis=-1, keepdims=True) + EPS_NORM)
    return centred * inverse, inverse


def norm_back(scaled, unit, inverse):
    return inverse * (
        scaled
        - jnp.mean(scaled, axis=-1, keepdims=True)
        - unit * jnp.mean(scaled * unit, axis=-1, keepdims=True)
    )


def column_to_row(column, width, offset):
    shape = (column.shape[0], width)
    hit = iota(shape, 0) == iota(shape, 1) + offset
    return jnp.sum(jnp.where(hit, column, 0.0), axis=0, keepdims=True)


def row_to_column(row, rows, offset):
    shape = (rows, row.shape[1])
    hit = iota(shape, 0) == iota(shape, 1) + offset
    return jnp.sum(jnp.where(hit, row, 0.0), axis=1, keepdims=True)


def token_hits(table_ref, chunk, rows, tokens):
    slot = iota((rows, LANES), 0)
    lane = iota((rows, LANES), 1)
    picked = jnp.zeros((rows, LANES), wide)
    for high in range((rows + HALF - 1) // HALF):
        line = table_ref[pl.ds(chunk * 8 + high, 1), :]
        picked = jnp.where(slot // HALF == high, line, picked)
    picked = jnp.where(slot % HALF == lane % HALF, picked, 0.0)
    picked = picked * jnp.where(lane < HALF, float(HALF), 1.0)
    token = jnp.sum(picked, axis=1, keepdims=True).astype(jnp.int32) - 1
    return jnp.where(token == iota((rows, tokens), 1), 1.0, 0.0).astype(lowp)


def seat_kernel(experts, cap, cap_rows, seq_rows,
                routes_ref, order_ref, cot_ref, slots_ref, table_ref, rows_ref,
                route_s, order_s, flat_s):
    images, seq, _ = routes_ref.shape
    tokens = images * seq_rows
    step = pl.program_id(0)

    @pl.when(step == 0)
    def _():
        route_s[...] = jnp.full(route_s.shape, -1, jnp.int32)
        order_s[...] = jnp.zeros(order_s.shape, jnp.int32)
        flat_s[...] = jnp.zeros(flat_s.shape, lowp)
        for image in range(images):
            rows = pl.ds(image * seq_rows, seq)
            route_s[rows, :] = routes_ref[image]
            order_s[rows, :] = order_ref[image]
            flat_s[rows, :] = cot_ref[image]
        lane = iota((tokens, LANES), 1)
        wide_lane = iota((tokens, experts * HALF), 1)
        route = [route_s[:, k : k + 1] for k in range(2)]
        order = [order_s[:, k : k + 1] for k in range(2)]
        low_hit = [(order[k] % HALF == lane % HALF) for k in range(2)]
        low_b = [jnp.where(low_hit[k], 1.0, 0.0).astype(lowp) for k in range(2)]
        high_b = [
            jnp.where((route[k] * HALF + order[k] // HALF) == wide_lane, 1.0, 0.0).astype(lowp)
            for k in range(2)
        ]
        counts = (dot_tn(low_b[0], high_b[0]) + dot_tn(low_b[1], high_b[1])).astype(lowp)
        before = iota((LANES, LANES), 0)
        after = iota((LANES, LANES), 1)
        upper = jnp.where((after < HALF) & (after < before % HALF), 1.0, 0.0).astype(lowp)
        within = dot(upper, counts)
        block = (experts * HALF, experts * HALF)
        earlier = jnp.where(
            (iota(block, 0) // HALF == iota(block, 1) // HALF) & (iota(block, 0) < iota(block, 1)),
            1.0, 0.0,
        ).astype(lowp)
        base = jnp.sum(dot(counts, earlier)[:HALF], axis=0, keepdims=True)
        place = within + base
        place_high = jnp.floor(place * (1.0 / HALF))
        place_low = place - place_high * HALF
        split = jnp.where(iota(place.shape, 0) < HALF, place_high, place_low).astype(lowp)
        weight = jnp.where(lane < HALF, float(HALF), 1.0)
        token = iota((tokens, LANES), 0) + 1
        table = jnp.zeros((experts * 8, LANES), wide)
        row = iota((tokens, experts * 8), 1)
        columns = iota((tokens, 4), 1)
        found = jnp.zeros((tokens, 4), jnp.int32)
        for k in range(2):
            gathered = dot_nt(high_b[k], split)
            position = jnp.sum(
                jnp.where(low_hit[k], gathered * weight, 0.0), axis=1, keepdims=True
            ).astype(jnp.int32)
            seated = (position < cap) & (route[k] >= 0)
            slot = jnp.where(seated, route[k] * cap_rows + position, -1)
            found = jnp.where(columns == k, slot, found)
            found = jnp.where(columns == 2 + k, route[k], found)
            which = jnp.where(seated, route[k] * 8 + position // HALF, -1)
            which_b = jnp.where(which == row, 1.0, 0.0).astype(lowp)
            value = jnp.where(lane < HALF, token // HALF, token % HALF).astype(wide)
            value_b = jnp.where(position % HALF == lane % HALF, value, 0.0).astype(lowp)
            table = table + dot_tn(which_b, value_b)
        table_ref[...] = table
        for image in range(images):
            slots_ref[image] = found[image * seq_rows : (image + 1) * seq_rows]

    hits = token_hits(table_ref, step, cap_rows, tokens)
    rows_ref[0] = dot(hits, flat_s[...]).astype(lowp)


def front_kernel(seq, experts,
                 me_ref, x_ref, noise_ref, vec_ref, wq_ref, wk_ref, wv_ref, wo_ref, wr_ref,
                 q_ref, k_ref, v_ref, lse_ref, mix_ref, state_ref, aug_ref, probs_ref,
                 x_s, noise_s):
    rows, width = x_s.shape

    @pl.when(pl.program_id(0) == 0)
    def _():
        x_s[...] = jnp.zeros(x_s.shape, wide)
        noise_s[...] = jnp.zeros(noise_s.shape, wide)

    x_s[0:seq, :] = x_ref[0].astype(wide)
    noise_s[0:seq, :] = noise_ref[0]
    x = x_s[...]
    unit, _ = unit_norm(x)
    normed = (unit * vec_ref[0:1, :] + vec_ref[1:2, :]).astype(lowp)
    head_size = width // HEADS
    query = (dot(normed, wq_ref[...]) + vec_ref[2:3, :]).astype(lowp)
    query = query * (head_size ** -0.5)
    key = dot(normed, wk_ref[...]).astype(lowp)
    value = (dot(normed, wv_ref[...]) + vec_ref[3:4, :]).astype(lowp)
    q_ref[0] = query
    k_ref[0] = key
    v_ref[0] = value
    live = iota((rows, rows), 1) < seq
    lane = iota((rows, LANES), 1)
    lse_all = jnp.zeros((rows, LANES), wide)
    mixed = []
    for pair in range(HEADS // 2):
        cols = slice(pair * LANES, (pair + 1) * LANES)
        q2, k2, v2 = query[:, cols], key[:, cols], value[:, cols]
        outs = []
        for half in range(2):
            mine = (lane < HALF) if half == 0 else (lane >= HALF)
            scores = dot_nt(jnp.where(mine, q2, jnp.zeros_like(q2)), k2)
            scores = jnp.where(live, scores, -1e30)
            peak = jnp.max(scores, axis=1, keepdims=True)
            expo = jnp.exp(scores - peak)
            total = jnp.sum(expo, axis=1, keepdims=True)
            lse_all = jnp.where(lane == pair * 2 + half, peak + jnp.log(total), lse_all)
            outs.append(dot((expo / total).astype(lowp), v2))
        mixed.append(jnp.where(lane < HALF, outs[0], outs[1]).astype(lowp))
    mixed = jnp.concatenate(mixed, axis=1)
    lse_ref[0] = lse_all
    mix_ref[0] = mixed
    state = x + dot(mixed, wo_ref[...]) + vec_ref[4:5, :]
    state_ref[0] = state
    unit_two, _ = unit_norm(state)
    routed = (unit_two * vec_ref[5:6, :] + vec_ref[6:7, :]).astype(lowp)
    logits = dot(routed, wr_ref[...]) + noise_s[...]
    top = jnp.max(logits, axis=1, keepdims=True)
    expo = jnp.exp(logits - top)
    probs = expo / jnp.sum(expo, axis=1, keepdims=True)
    probs_ref[0] = probs
    me = me_ref[0]
    shape = (experts, LANES)
    swap = jnp.where(iota(shape, 0) == (iota(shape, 1) ^ me), 1.0, 0.0).astype(lowp)
    aug_ref[0, :, 0:width] = routed
    aug_ref[0, :, width : width + LANES] = dot(probs.astype(lowp), swap).astype(lowp)


def send_kernel(cap, gate_rows, table_ref, aug_ref, out_ref):
    _, cap_rows, width = out_ref.shape
    tokens = aug_ref.shape[0]
    chunk = pl.program_id(0)
    hits = token_hits(table_ref, chunk, cap_rows, tokens)
    full = dot(hits, aug_ref[...])
    rows = full[:, 0:width]
    lane = iota((cap_rows, LANES), 1)
    gate = jnp.sum(jnp.where(lane == chunk, full[:, width:], 0.0), axis=1, keepdims=True)
    at = iota((cap_rows, width), 0)
    for part in range(gate_rows):
        line = column_to_row(gate, width, part * width)
        rows = jnp.where(at == cap + part, line, rows)
    out_ref[0] = rows.astype(lowp)


def expert_kernel(cap, gate_rows, blocks, x_ref, g_ref, win_ref, wout_ref,
                  back_ref, prod_ref, act_ref, pre_ref, slot_ref):
    _, cap_rows, width = x_ref.shape
    inner = win_ref.shape[1]
    x = x_ref[0]
    grad = g_ref[0].astype(wide)
    gate = jnp.zeros((cap_rows, 1), wide)
    for part in range(gate_rows):
        line = x_ref[0, cap + part : cap + part + 1, :].astype(wide)
        gate = gate + row_to_column(line, cap_rows, part * width)
    gate = jnp.where(iota((cap_rows, 1), 0) < cap, gate, 0.0)
    slot_grad = (gate * grad).astype(lowp)
    slot_ref[...] = slot_grad
    made = jnp.zeros((cap_rows, width), wide)
    back = jnp.zeros((cap_rows, width), wide)
    size = inner // blocks
    outer = (2.0 / jnp.pi) ** 0.5
    for block in range(blocks):
        cols = slice(block * size, (block + 1) * size)
        win = win_ref[:, cols]
        wout = wout_ref[cols, :]
        pre = dot(x, win)
        hidden = dot_nt(slot_grad, wout)
        square = pre * pre
        angle = pre * (outer + (outer * 0.044715) * square)
        half = 0.5 * jnp.tanh(angle) + 0.5
        act = (pre * half).astype(lowp)
        slope = half * (
            1.0 + (1.0 - half) * (pre * (2.0 * outer + (6.0 * outer * 0.044715) * square))
        )
        pre_grad = (hidden * slope).astype(lowp)
        act_ref[:, cols] = act
        pre_ref[:, cols] = pre_grad
        made = made + dot(act, wout)
        back = back + dot_nt(pre_grad, win)
    made_b = made.astype(lowp)
    prod_ref[0] = made_b
    gate_grad = jnp.sum(grad * made_b.astype(wide), axis=1, keepdims=True)
    at = iota((cap_rows, width), 0)
    for part in range(gate_rows):
        line = column_to_row(gate_grad, width, part * width)
        high = line.astype(lowp).astype(wide)
        back = jnp.where(at == cap + part, high, back)
        back = jnp.where(at == cap + gate_rows + part, line - high, back)
    back_ref[0] = back.astype(lowp)


def weight_kernel(x_ref, slot_ref, act_ref, pre_ref, din_ref, dout_ref, in_s, out_s):
    step = pl.program_id(0)

    @pl.when(step == 0)
    def _():
        in_s[...] = jnp.zeros(in_s.shape, wide)
        out_s[...] = jnp.zeros(out_s.shape, wide)

    in_s[...] += dot_tn(x_ref[...], pre_ref[...])
    out_s[...] += dot_tn(slot_ref[...], act_ref[...])

    @pl.when(step == pl.num_programs(0) - 1)
    def _():
        din_ref[...] = in_s[...].astype(lowp)
        dout_ref[...] = out_s[...].T.astype(lowp)


def slot_hits(slots_ref, shape):
    at = iota(shape, 1)
    return slots_ref[0, :, 0:1] == at, slots_ref[0, :, 1:2] == at


def back_kernel(seq, experts, cap, cap_rows, gate_rows,
                me_ref, slots_ref, x_ref, cot_ref, q_ref, k_ref, v_ref, lse_ref, mix_ref,
                state_ref, probs_ref, vec_ref, rows_ref, wq_ref, wk_ref, wv_ref, wo_ref, wr_ref,
                grad_ref, sums_ref, small_ref,
                x_s, cot_s, aug_s):
    step = pl.program_id(0)
    rows, width = x_s.shape
    slot_total = experts * cap_rows

    @pl.when(step == 0)
    def _():
        x_s[...] = jnp.zeros(x_s.shape, wide)
        cot_s[...] = jnp.zeros(cot_s.shape, wide)
        sums_ref[...] = jnp.zeros(sums_ref.shape, wide)
        small_ref[...] = jnp.zeros(small_ref.shape, wide)

        @pl.loop(0, experts)
        def _(chunk):
            lane = iota((cap_rows, LANES), 1)
            extra = jnp.zeros((cap_rows, LANES), wide)
            for part in range(gate_rows):
                for piece in range(2):
                    line = rows_ref[chunk, cap + piece * gate_rows + part :
                                    cap + piece * gate_rows + part + 1, :].astype(wide)
                    column = row_to_column(line, cap_rows, part * width)
                    extra = jnp.where(lane == chunk + piece * HALF, extra + column, extra)
            at = pl.ds(pl.multiple_of(chunk * cap_rows, 16), cap_rows)
            aug_s[at, 0:width] = rows_ref[chunk]
            aug_s[at, width : width + LANES] = extra.astype(lowp)

    x_s[0:seq, :] = x_ref[0].astype(wide)
    cot_s[0:seq, :] = cot_ref[0].astype(wide)
    first, second = slot_hits(slots_ref, (rows, slot_total))
    hits = jnp.where(first | second, 1.0, 0.0).astype(lowp)
    full = dot(hits, aug_s[...])
    me = me_ref[0]
    shape = (LANES, experts)
    swap = jnp.where((iota(shape, 0) % HALF) == (iota(shape, 1) ^ me), 1.0, 0.0).astype(lowp)
    prob_grad = dot(full[:, width:].astype(lowp), swap)
    probs = probs_ref[0]
    logit_grad = (
        probs * (prob_grad - jnp.sum(probs * prob_grad, axis=1, keepdims=True))
    ).astype(lowp)
    routed_grad = full[:, 0:width] + dot_nt(logit_grad, wr_ref[...])
    unit_two, inverse_two = unit_norm(state_ref[0])
    gain_two = vec_ref[5:6, :]
    routed = (unit_two * gain_two + vec_ref[6:7, :]).astype(lowp)
    router_grad = dot_tn(logit_grad, routed)
    state_grad = cot_s[...] + norm_back(routed_grad * gain_two, unit_two, inverse_two)
    branch = state_grad.astype(lowp)
    mixed_grad = dot_nt(branch, wo_ref[...]).astype(lowp)
    sums_ref[3 * width : 4 * width, :] += dot_tn(mix_ref[0], branch)

    query, key, value = q_ref[0], k_ref[0], v_ref[0]
    lse = lse_ref[0]
    live = iota((rows, rows), 1) < seq
    lane = iota((rows, LANES), 1)
    scale = (width // HEADS) ** -0.5
    parts = [[], [], []]
    for pair in range(HEADS // 2):
        cols = slice(pair * LANES, (pair + 1) * LANES)
        q2, k2, v2, g2 = query[:, cols], key[:, cols], value[:, cols], mixed_grad[:, cols]
        outs = [[], [], []]
        for half in range(2):
            mine = (lane < HALF) if half == 0 else (lane >= HALF)
            scores = dot_nt(jnp.where(mine, q2, jnp.zeros_like(q2)), k2)
            head = pair * 2 + half
            weights = jnp.exp(jnp.where(live, scores - lse[:, head : head + 1], -1e30))
            weight_grad = dot_nt(jnp.where(mine, g2, jnp.zeros_like(g2)), v2)
            product = weights * weight_grad
            score_grad = (
                product - weights * jnp.sum(product, axis=1, keepdims=True)
            ).astype(lowp)
            outs[0].append(dot(score_grad, k2))
            outs[1].append(dot_tn(score_grad, q2))
            outs[2].append(dot_tn(weights.astype(lowp), g2))
        for which in range(3):
            joined = jnp.where(lane < HALF, outs[which][0], outs[which][1])
            if which == 0:
                joined = joined * scale
            parts[which].append(joined.astype(lowp))
    query_grad, key_grad, value_grad = (jnp.concatenate(p, axis=1) for p in parts)
    unit_one, inverse_one = unit_norm(x_s[...])
    gain_one = vec_ref[0:1, :]
    normed = (unit_one * gain_one + vec_ref[1:2, :]).astype(lowp)
    sums_ref[0:width, :] += dot_tn(normed, query_grad)
    sums_ref[width : 2 * width, :] += dot_tn(normed, key_grad)
    sums_ref[2 * width : 3 * width, :] += dot_tn(normed, value_grad)
    normed_grad = (
        dot_nt(query_grad, wq_ref[...])
        + dot_nt(key_grad, wk_ref[...])
        + dot_nt(value_grad, wv_ref[...])
    )
    result = state_grad + norm_back(normed_grad * gain_one, unit_one, inverse_one)
    grad_ref[0] = result.astype(lowp)[0:seq]
    lines = [
        query_grad.astype(wide),
        value_grad.astype(wide),
        branch.astype(wide),
        normed_grad * unit_one,
        normed_grad,
        routed_grad * unit_two,
        routed_grad,
    ]
    small = jnp.concatenate(
        [jnp.sum(line, axis=0, keepdims=True) for line in lines]
        + [jnp.zeros((1, width), wide)], axis=0
    )
    small_ref[0:8, :] += small
    small_ref[8 : 8 + experts, :] += router_grad


def out_kernel(slots_ref, aug_ref, state_ref, rows_ref, out_ref):
    _, rows, width = state_ref.shape
    seq = out_ref.shape[1]
    slot_total = rows_ref.shape[0]
    lane = iota((rows, LANES), 1)
    gates = aug_ref[0, :, width : width + LANES].astype(wide)
    gate = [
        jnp.sum(jnp.where(lane == slots_ref[0, :, 2 + k : 3 + k], gates, 0.0), axis=1, keepdims=True)
        for k in range(2)
    ]
    first, second = slot_hits(slots_ref, (rows, slot_total))
    hits = jnp.where(first, gate[0], jnp.where(second, gate[1], 0.0)).astype(lowp)
    out_ref[0] = (state_ref[0] + dot(hits, rows_ref[...])).astype(lowp)[0:seq]


def adam_step(master, moment, second, grad):
    new_moment = BETA_ONE * moment + (1.0 - BETA_ONE) * grad
    new_second = BETA_TWO * second + (1.0 - BETA_TWO) * grad * grad
    corr_one = 1.0 - BETA_ONE**adam_steps
    corr_two = 1.0 - BETA_TWO**adam_steps
    update = LEARN_RATE * (new_moment / corr_one) / (jnp.sqrt(new_second / corr_two) + ADAM_EPS)
    return (master - update, new_moment, new_second)


def whole(shape):
    return pl.BlockSpec(shape, lambda i: (0,) * len(shape))


def one(shape):
    return pl.BlockSpec((1,) + shape, lambda i: (i,) + (0,) * len(shape))


def smem():
    return pl.BlockSpec(memory_space=pltpu.SMEM)


def like(shape, dtype):
    return jax.ShapeDtypeStruct(shape, dtype)


def sum_all(values, n_expert, n_dp):
    rows, width = values.shape
    part = rows // n_expert
    pieces = lax.all_to_all(
        values.reshape(n_expert, part, width), "expert", split_axis=0, concat_axis=0, tiled=True
    )
    mine = jnp.sum(pieces.astype(wide), axis=0).astype(lowp)
    others = [
        lax.ppermute(mine, "dp", [(i, (i + shift) % n_dp) for i in range(n_dp)])
        for shift in range(1, n_dp)
    ]
    total = mine.astype(wide)
    for other in others:
        total = total + other.astype(wide)
    return lax.all_gather(total.astype(lowp), "expert", axis=0, tiled=True)


def on_device(n_expert, n_dp, images, cotangent, router_noise, routes, seat_order,
              norm1_gain, norm1_shift, query_weight, query_bias, key_weight, value_weight,
              value_bias, output_weight, output_bias, norm2_gain, norm2_shift, router_weight,
              expert_in, expert_out, master_in, master_out, moment_in, moment_out,
              second_in, second_out):
    count, seq, width = images.shape
    experts = router_noise.shape[2]
    cap = (count * seq * 2 + experts - 1) // experts
    gate_rows = (cap + width - 1) // width
    cap_rows = round_up(cap + 2 * gate_rows, 16)
    seq_rows = round_up(seq, 16)
    tokens = count * seq_rows
    inner = expert_in.shape[2]
    slot_total = experts * cap_rows
    aug = width + LANES
    me = jnp.zeros((1,), jnp.int32)
    vecs = jnp.stack([norm1_gain, norm1_shift, query_bias, value_bias, output_bias,
                      norm2_gain, norm2_shift, norm2_shift])

    slots, table, grad_rows = pl.pallas_call(
        functools.partial(seat_kernel, experts, cap, cap_rows, seq_rows),
        grid=(experts,),
        in_specs=[whole(routes.shape), whole(routes.shape), whole(cotangent.shape)],
        out_specs=[whole((count, seq_rows, 4)), whole((experts * 8, LANES)),
                   one((cap_rows, width))],
        out_shape=[like((count, seq_rows, 4), jnp.int32), like((experts * 8, LANES), wide),
                   like((experts, cap_rows, width), lowp)],
        scratch_shapes=[pltpu.VMEM((tokens, 2), jnp.int32), pltpu.VMEM((tokens, 2), jnp.int32),
                        pltpu.VMEM((tokens, width), lowp)],
        compiler_params=params(1),
        name="seat",
    )(routes, seat_order.reshape(routes.shape), cotangent)
    grad_in = lax.all_to_all(grad_rows, "expert", split_axis=0, concat_axis=0, tiled=True)

    square = (width, width)
    token_shape = (count, seq_rows, width)
    query, key, value, lse, mixed, state, routed, probs = pl.pallas_call(
        functools.partial(front_kernel, seq, experts),
        grid=(count,),
        in_specs=[smem(), one((seq, width)), one((seq, experts)), whole((8, width)),
                  whole(square), whole(square), whole(square), whole(square),
                  whole((width, experts))],
        out_specs=[one((seq_rows, width))] * 3 + [
            one((seq_rows, LANES)), one((seq_rows, width)), one((seq_rows, width)),
            one((seq_rows, aug)), one((seq_rows, experts))],
        out_shape=[like(token_shape, lowp)] * 3 + [
            like((count, seq_rows, LANES), wide), like(token_shape, lowp),
            like(token_shape, wide), like((count, seq_rows, aug), lowp),
            like((count, seq_rows, experts), wide)],
        scratch_shapes=[pltpu.VMEM((seq_rows, width), wide),
                        pltpu.VMEM((seq_rows, experts), wide)],
        compiler_params=params(1),
        name="front",
    )(me, images, router_noise, vecs, query_weight, key_weight, value_weight, output_weight,
      router_weight)

    sent = pl.pallas_call(
        functools.partial(send_kernel, cap, gate_rows),
        grid=(experts,),
        in_specs=[whole((experts * 8, LANES)), whole((tokens, aug))],
        out_specs=one((cap_rows, width)),
        out_shape=like((experts, cap_rows, width), lowp),
        compiler_params=params(1),
        name="send",
    )(table, routed.reshape(tokens, aug))
    sent, grad_in = lax.optimization_barrier((sent, grad_in))
    arrived = lax.all_to_all(sent, "expert", split_axis=0, concat_axis=0, tiled=True)

    back, produced, act, pre_grad, slot_grad = pl.pallas_call(
        functools.partial(expert_kernel, cap, gate_rows, 3),
        grid=(experts,),
        in_specs=[one((cap_rows, width)), one((cap_rows, width)), whole((width, inner)),
                  whole((inner, width))],
        out_specs=[one((cap_rows, width)), one((cap_rows, width)),
                   pl.BlockSpec((cap_rows, inner), lambda i: (i, 0)),
                   pl.BlockSpec((cap_rows, inner), lambda i: (i, 0)),
                   pl.BlockSpec((cap_rows, width), lambda i: (i, 0))],
        out_shape=[like((experts, cap_rows, width), lowp), like((experts, cap_rows, width), lowp),
                   like((slot_total, inner), lowp), like((slot_total, inner), lowp),
                   like((slot_total, width), lowp)],
        compiler_params=params(1),
        name="expert",
    )(arrived, grad_in, expert_in[0], expert_out[0])

    back_rows = lax.all_to_all(back, "expert", split_axis=0, concat_axis=0, tiled=True)

    steps = 4
    per = slot_total // steps
    row_block = lambda size: pl.BlockSpec((per, size), lambda i: (i, 0))
    grad_weight_in, grad_weight_out = pl.pallas_call(
        weight_kernel,
        grid=(steps,),
        in_specs=[row_block(width), row_block(width), row_block(inner), row_block(inner)],
        out_specs=[whole((width, inner)), whole((inner, width))],
        out_shape=[like((width, inner), lowp), like((inner, width), lowp)],
        scratch_shapes=[pltpu.VMEM((width, inner), wide), pltpu.VMEM((width, inner), wide)],
        compiler_params=params(1),
        name="weight",
    )(arrived.reshape(slot_total, width), slot_grad, act, pre_grad)

    back_rows, grad_weight_in, grad_weight_out = lax.optimization_barrier(
        (back_rows, grad_weight_in, grad_weight_out))
    share_in = lax.psum_scatter(grad_weight_in[None], "dp", scatter_dimension=1, tiled=True)
    share_out = lax.psum_scatter(grad_weight_out[None], "dp", scatter_dimension=1, tiled=True)
    returned = lax.all_to_all(produced, "expert", split_axis=0, concat_axis=0, tiled=True)

    small_rows = 8 + round_up(experts, 8)
    images_grad, sums, small = pl.pallas_call(
        functools.partial(back_kernel, seq, experts, cap, cap_rows, gate_rows),
        grid=(count,),
        in_specs=[smem(), one((seq_rows, 4)), one((seq, width)), one((seq, width))]
        + [one((seq_rows, width))] * 3
        + [one((seq_rows, LANES)), one((seq_rows, width)), one((seq_rows, width)),
           one((seq_rows, experts)), whole((8, width)), whole((experts, cap_rows, width)),
           whole(square), whole(square), whole(square), whole(square), whole((width, experts))],
        out_specs=[one((seq, width)), whole((4 * width, width)), whole((small_rows, width))],
        out_shape=[like(images.shape, lowp), like((4 * width, width), wide),
                   like((small_rows, width), wide)],
        scratch_shapes=[pltpu.VMEM((seq_rows, width), wide), pltpu.VMEM((seq_rows, width), wide),
                        pltpu.VMEM((slot_total, aug), lowp)],
        compiler_params=params(1),
        name="back",
    )(me, slots, images, cotangent, query, key, value, lse, mixed, state, probs, vecs, back_rows,
      query_weight, key_weight, value_weight, output_weight, router_weight)

    block_out = pl.pallas_call(
        out_kernel,
        grid=(count,),
        in_specs=[one((seq_rows, 4)), one((seq_rows, aug)), one((seq_rows, width)),
                  whole((slot_total, width))],
        out_specs=one((seq, width)),
        out_shape=like(images.shape, lowp),
        compiler_params=params(1),
        name="block_out",
    )(slots, routed, state, returned.reshape(slot_total, width))

    small_high = small.astype(lowp)
    small_low = (small - small_high.astype(wide)).astype(lowp)
    packed = jnp.concatenate([sums.astype(lowp), small_high, small_low], axis=0)
    packed_rows = packed.shape[0]
    packed = jnp.pad(packed, ((0, round_up(packed_rows, 16 * n_expert) - packed_rows), (0, 0)))
    total = sum_all(packed, n_expert, n_dp)
    big = total[0 : 4 * width].astype(wide).reshape(4, width, width)
    small_sum = (total[4 * width : 4 * width + small_rows].astype(wide)
                 + total[4 * width + small_rows : 4 * width + 2 * small_rows].astype(wide))

    new_master_in, new_moment_in, new_second_in = adam_step(
        master_in, moment_in, second_in, share_in.astype(wide))
    new_master_out, new_moment_out, new_second_out = adam_step(
        master_out, moment_out, second_out, share_out.astype(wide))
    new_expert_in = lax.all_gather(new_master_in.astype(lowp), "dp", axis=1, tiled=True)
    new_expert_out = lax.all_gather(new_master_out.astype(lowp), "dp", axis=1, tiled=True)
    return (
        block_out,
        images_grad,
        small_sum[3],
        small_sum[4],
        big[0],
        small_sum[0],
        big[1],
        big[2],
        small_sum[1],
        big[3],
        small_sum[2],
        small_sum[5],
        small_sum[6],
        small_sum[8 : 8 + experts].T,
        new_expert_in,
        new_expert_out,
        new_master_in,
        new_master_out,
        new_moment_in,
        new_moment_out,
        new_second_in,
        new_second_out,
    )


def solution(mesh):
    both = ("dp", "expert")
    in_specs = (
        (P(both, None, None),) * 4
        + (P(both, None),)
        + (P(),) * 12
        + (P("expert", None, None),) * 2
        + (P("expert", "dp", None),) * 6
    )
    out_specs = (
        (P(both, None, None),) * 2
        + (P(),) * 12
        + (P("expert", None, None),) * 2
        + (P("expert", "dp", None),) * 6
    )
    body = functools.partial(on_device, mesh.shape["expert"], mesh.shape["dp"])
    return jax.shard_map(body, mesh=mesh, in_specs=in_specs, out_specs=out_specs, check_vma=False)
```

time: 647 us -> 372 us (0.57); the launches traced: 636 us -> 371 us
  matrix products: 185 us -> 0 us
  Pallas kernels: 0 us -> 155 us
  local copies, waits for them, and re-layouts: 130 us -> 21.2 us
  other arithmetic: 70.8 us -> 11.8 us
  blocking collectives: 112 us -> 55.1 us
  waiting for transfers between devices: 113 us -> 94 us
  starting transfers between devices: 9.51 us -> 17.9 us
    dot_general x33 -> x0, matrix products: 185 us -> none  [the longest x7 40.9 us: contract_cols(): lax.dot_general(left, right, (((1,), (1,)), ((), ())), preferred_element_...]
    pallas_call x0 -> x7, Pallas kernels: none -> 155 us  [the longest x1 46 us: on_device(): pl.pallas_call(functools.partial(back_kernel, seq, experts, cap, cap_rows...]
    reshape x25 -> x1, local copies, waits for them, and re-layouts: 79.3 us -> 1.2 us  [on_device(): seat_order.reshape(routes.shape)]
    psum x1 -> x0, waiting for transfers between devices: 76.2 us -> none  [on_device(): lax.psum((weight_stack, small_stack), ('dp', 'expert'))]
    psum x1 -> x0, blocking collectives: 41.5 us -> none  [on_device(): lax.psum((weight_stack, small_stack), ('dp', 'expert'))]
    all_gather x1, waiting for transfers between devices: 0.01 us -> 31.5 us  [on_device(): lax.all_gather(new_master_in.astype(lowp), 'dp', axis=1, tiled=True)]
    reduce_sum x9 -> x1, other arithmetic: 26.2 us -> 0.18 us  [sum_all(): mine = jnp.sum(pieces.astype(wide), axis=0).astype(lowp)]
    convert_element_type x9 -> x4, other arithmetic: 22.3 us -> 4.01 us  [the longest x1 1.81 us: on_device(): packed = jnp.concatenate([sums.astype(lowp), small_high, small_low], axis=0)]
  transfers between devices with their start and end apart: 7 -> 11, of which waited for: 3 -> 6; matrix products, arithmetic and copies ran while one was open for 24% -> 6% of each run, Pallas kernels for 0% -> 26%
where the time goes in v1:
time: 372 us; the launch traced here: 371 us
  Pallas kernels  155 us (42%)
  waiting for transfers between devices  94 us (25%)
  blocking collectives  55.1 us (15%)
  local copies, waits for them, and re-layouts  21.2 us (6%)
  starting transfers between devices  17.9 us (5%)
  between operations  16 us (4%)
  other arithmetic  11.8 us (3%)
    pallas_call x1, Pallas kernels, on_device(): pl.pallas_call(functools.partial(back_kernel, seq, experts, cap, cap_rows...  46 us
    all_to_all x1, blocking collectives, on_device(): lax.all_to_all(sent, 'expert', split_axis=0, concat_axis=0, tiled=True)  34.9 us
    all_gather x1, waiting for transfers between devices, on_device(): lax.all_gather(new_master_in.astype(lowp), 'dp', axis=1, tiled=True)  31.5 us
    pallas_call x1, Pallas kernels, on_device(): pl.pallas_call(functools.partial(expert_kernel, cap, gate_rows, 3), grid=...  29.7 us
    all_to_all x1, waiting for transfers between devices, on_device(): lax.all_to_all(produced, 'expert', split_axis=0, concat_axis=0, tiled=True)  29.4 us
    pallas_call x1, Pallas kernels, on_device(): pl.pallas_call(functools.partial(front_kernel, seq, experts), grid=(count...  20.5 us
    all_to_all x1, blocking collectives, sum_all(): lax.all_to_all(values.reshape(n_expert, part, width), 'expert', split_axi...  20.2 us
    pallas_call x1, Pallas kernels, on_device(): pl.pallas_call(functools.partial(seat_kernel, experts, cap, cap_rows, seq...  18.7 us
  transfers between devices with their start and end apart: 11, of which 6 were waited for; matrix products, arithmetic and copies ran while one was open for 6% of the time, Pallas kernels for 26%

profile of v1, /device:TPU:0, one launch (start us, length us, event | category | flops | bytes accessed | tf_op | source)
XLA Modules:
  0.0 371.0 jit_solution(11990904397168649306)
XLA Ops:
  13.2 18.7 %seat.1 = (s32[8,208,4]{2,1,0:T(8,128)}, f32[64,128]{1,0:T(8,128)}, bf16[8,400,384]{2,1,0:T(8,128)(2,1)}) custom-call(s32[8,197,2]{2,1,0:T(8,128)} %copy.57.routes_ref, s32[8,197,2]{2,1,0:T(8,128)} %reshape.68.order_ref, bf16[8,197,384]{2,1,0:T(8,128)(2,1)} %copy.58.cot_ref), custom_call_target="tpu_custom_call" | custom-call | tf_op jit(solution)/shard_map/seat/pallas_call | solution.py:495
  32.0 5.3 %all-to-all-start = ((bf16[8,400,384]{2,1,0:T(8,128)(2,1)}), bf16[8,400,384]{2,1,0:T(8,128)(2,1)S(1)}, u32[]{:S(2)}, u32[]{:S(2)}) async-start(bf16[8,400,384]{2,1,0:T(8,128)(2,1)} %get-tuple-element.52), calls=%async_computation | async-start | bytes 4915200 | tf_op jit(solution)/shard_map/all_to_all | solution.py:508
  39.4 2.5 copy.59.x_ref
  42.5 20.5 %front.1 = (bf16[8,208,384]{2,1,0:T(8,128)(2,1)}, bf16[8,208,384]{2,1,0:T(8,128)(2,1)}, bf16[8,208,384]{2,1,0:T(8,128)(2,1)}, f32[8,208,128]{2,1,0:T(8,128)}, bf...) custom-call(s32[1]{0:T(128)} %constant.9.clone.1.me_ref, ...), custom_call_target="tpu_custom_call" | custom-call | tf_op jit(solution)/shard_map/front/pallas_call | solution.py:512
  63.1 10.7 %send.1 = bf16[8,400,384]{2,1,0:T(8,128)(2,1)} custom-call(f32[64,128]{1,0:T(8,128)} %get-tuple-element.51.table_ref, bf16[1664,512]{1,0:T(8,128)(2,1)} %bitcast.12), custom_call_target="tpu_custom_call" | custom-call | tf_op jit(solution)/shard_map/send/pallas_call | solution.py:532
  73.8 34.9 %all_to_all.25.x_ref = bf16[8,400,384]{2,1,0:T(8,128)(2,1)} all-to-all(bf16[8,400,384]{2,1,0:T(8,128)(2,1)} %send.1), channel_id=1, replica_groups=mesh['dp'=4,'expert'=8] {'expert'}, dimensions={0} | all-to-all | bytes 4915200 | tf_op jit(solution)/shard_map/all_to_all | solution.py:542
  108.7 29.7 %expert.1 = (bf16[8,400,384]{2,1,0:T(8,128)(2,1)}, bf16[8,400,384]{2,1,0:T(8,128)(2,1)}, bf16[3200,1536]{1,0:T(8,128)(2,1)}, bf16[3200,1536]{1,0:T(8,128)(2,1)}, bf16[3200,384]{1,0:T(8,128)(2,1)}) custom-call(bf16[8,400,384]{2,1,0:T(8,128)(2,1)} %all_to_all.25.x_ref, bf16[8,400,384]{2,1,0:T(8,128)(2,1)} %copy-done, bf16[384,1536]{1,0:T(8,128)(2,1)} %bitcast.14, ...), custom_call_target="tpu_custom_call" | custom-call | tf_op jit(solution)/shard_map/expert/pallas_call | solution.py:544
  138.4 3.6 all-to-all-start.3
  142.1 15.8 %weight.1 = (bf16[384,1536]{1,0:T(8,128)(2,1)}, bf16[1536,384]{1,0:T(8,128)(2,1)}) custom-call(bf16[3200,384]{1,0:T(8,128)(2,1)} %bitcast.10, bf16[3200,384]{1,0:T(8,128)(2,1)} %get-tuple-element.63.slot_ref, bf16[3200,1536]{1,0:T(8,128)(2,1)} %get-tuple-element.64.act_ref, bf16[3200,1536]{1,0:T(8,128)(2,1)} %get-tuple-element.65.pre_ref), custom_call_target="tpu_custom_call" | custom-call | tf_op jit(solution)/shard_map/weight/pallas_call | solution.py:565
  157.9 14.6 %all-to-all-done.3.rows_ref = bf16[8,400,384]{2,1,0:T(8,128)(2,1)S(1)} async-done(((bf16[8,400,384]{2,1,0:T(8,128)(2,1)}), bf16[8,400,384]{2,1,0:T(8,128)(2,1)S(1)}, u32[]{:S(2)}, u32[]{:S(2)}) %all-to-all-start.3) | async-done | bytes 2457632 | tf_op jit(solution)/shard_map/all_to_all | solution.py:560
  174.0 46.0 %back.1 = (bf16[8,197,384]{2,1,0:T(8,128)(2,1)}, f32[1536,384]{1,0:T(8,128)}, f32[16,384]{1,0:T(8,128)}) custom-call(s32[1]{0:T(128)} %constant.9.clone.1.me_ref, s32[8,208,4]{2,1,0:T(8,128)} %get-tuple-element.48.slots_ref, bf16[8,197,384]{2,1,0:T(8,128)(2,1)} %copy.59.x_ref, bf16[8,197,384]{2,1,0:T(8,128)(2,1)} %copy.58.cot_ref, ...), custom_call_target="tpu_custom_call" | custom-call | tf_op jit(solution)/shard_map/back/pallas_call | solution.py:583
  221.9 20.2 %all_to_all.26 = bf16[8,208,384]{2,1,0:T(8,128)(2,1)S(1)} all-to-all(bf16[8,208,384]{2,1,0:T(8,128)(2,1)S(1)} %bitcast.13), channel_id=1, replica_groups=mesh['dp'=4,'expert'=8] {'expert'}, dimensions={0} | all-to-all | bytes 2555904 | tf_op jit(solution)/shard_map/all_to_all | solution.py:462
  242.4 3.8 %collective-permute-start.2 = (bf16[208,384]{1,0:T(8,128)(2,1)S(1)}, bf16[208,384]{1,0:T(8,128)(2,1)S(1)}, u32[]{:S(2)}, u32[]{:S(2)}) collective-permute-start(bf16[208,384]{1,0:T(8,128)(2,1)S(1)} %reduce_sum.12), channel_id=1, source_target_pairs={{0,24},{8,0},{16,8},{24,16},{1,25},{9,1},{17,9},{25,17},{2,26},{10... | collective-permute-start | bytes 479240 | tf_op jit(solution)/shard_map/ppermute | solution.py:467
  247.1 3.6 collective-permute-done.2
  250.7 8.5 %collective-permute-done.1 = bf16[208,384]{1,0:T(8,128)(2,1)S(1)} collective-permute-done((bf16[208,384]{1,0:T(8,128)(2,1)S(1)}, bf16[208,384]{1,0:T(8,128)(2,1)S(1)}, u32[]{:S(2)}, u32[]{:S(2)}) %collective-permute-start.1) | collective-permute-done | bytes 159776 | tf_op jit(solution)/shard_map/ppermute | solution.py:467
  259.9 3.8 %all-to-all-start.2 = ((bf16[8,400,384]{2,1,0:T(8,128)(2,1)}), bf16[8,400,384]{2,1,0:T(8,128)(2,1)S(1)}, u32[]{:S(2)}, u32[]{:S(2)}) async-start(bf16[8,400,384]{2,1,0:T(8,128)(2,1)} %get-tuple-element.55), calls=%async_computation.2 | async-start | bytes 4915200 | tf_op jit(solution)/shard_map/all_to_all | solution.py:580
  263.8 2.9 fusion.9
  266.8 3.1 fusion.12
  269.9 29.4 %all-to-all-done.2 = bf16[8,400,384]{2,1,0:T(8,128)(2,1)S(1)} async-done(((bf16[8,400,384]{2,1,0:T(8,128)(2,1)}), bf16[8,400,384]{2,1,0:T(8,128)(2,1)S(1)}, u32[]{:S(2)}, u32[]{:S(2)}) %all-to-all-start.2) | async-done | bytes 2457632 | tf_op jit(solution)/shard_map/all_to_all | solution.py:580
  300.8 13.6 %block_out.1 = bf16[8,197,384]{2,1,0:T(8,128)(2,1)} custom-call(s32[8,208,4]{2,1,0:T(8,128)} %get-tuple-element.48.slots_ref, bf16[8,208,512]{2,1,0:T(8,128)(2,1)} %get-tuple-element.49.aug_ref, f32[8,208,384]{2,1,0:T(8,128)} %get-tuple-element.50.state_ref, bf16[3200,384]{1,0:T(8,128)(2,1)} %bitcast.11), custom_call_target="tpu_custom_call" | custom-call | tf_op jit(solution)/shard_map/block_out/pallas_call | solution.py:601
  314.3 2.6 copy.65
  322.9 5.6 %all-gather.8.cloned.1.call-done = bf16[1,1536,384]{2,1,0:T(8,128)(2,1)} async-done(((bf16[1,384,384]{2,1,0:T(8,128)(2,1)}), bf16[1,1536,384]{2,1,0:T(8,128)(2,1)}) %all-gather.8.cloned.1.call-update) | async-done | bytes 1179664 | tf_op jit(solution)/shard_map/all_gather | solution.py:627
  328.5 31.5 %all-gather.6.cloned.1.call-done = bf16[1,384,1536]{2,1,0:T(8,128)(2,1)} async-done(((bf16[1,96,1536]{2,1,0:T(8,128)(2,1)}), bf16[1,384,1536]{2,1,0:T(8,128)(2,1)}) %all-gather.6.cloned.1.call-update) | async-done | bytes 1179664 | tf_op jit(solution)/shard_map/all_gather | solution.py:626
  360.0 2.4 copy.69
  (77 shorter events, 21.9 us)
Async XLA Ops:
  8.0 4.0 %copy-start.4 = (bf16[8,197,384]{2,0,1:T(8,128)(2,1)S(1)}, bf16[8,197,384]{2,0,1:T(8,128)(2,1)}, u32[]{:S(2)}) copy-start(bf16[8,197,384]{2,0,1:T(8,128)(2,1)} %param.26) | copy-start | bytes 3631108
  31.9 5.4 %copy-start.10 = (f32[384]{0:T(512)S(1)}, f32[384]{0:T(512)}, u32[]{:S(2)}) copy-start(f32[384]{0:T(512)} %param.30) | copy-start | bytes 4612
  31.9 5.4 %copy-start.11 = (f32[384]{0:T(512)S(1)}, f32[384]{0:T(512)}, u32[]{:S(2)}) copy-start(f32[384]{0:T(512)} %param.31) | copy-start | bytes 4612
  31.9 5.4 %copy-start.12 = (f32[384]{0:T(512)S(1)}, f32[384]{0:T(512)}, u32[]{:S(2)}) copy-start(f32[384]{0:T(512)} %param.33) | copy-start | bytes 4612
  31.9 5.4 %copy-start.13 = (f32[384]{0:T(512)S(1)}, f32[384]{0:T(512)}, u32[]{:S(2)}) copy-start(f32[384]{0:T(512)} %param.36) | copy-start | bytes 4612
  31.9 5.5 %copy-start.14 = (f32[384]{0:T(512)S(1)}, f32[384]{0:T(512)}, u32[]{:S(2)}) copy-start(f32[384]{0:T(512)} %param.38) | copy-start | bytes 4612
  31.9 5.5 %copy-start.15 = (f32[384]{0:T(512)S(1)}, f32[384]{0:T(512)}, u32[]{:S(2)}) copy-start(f32[384]{0:T(512)} %param.39) | copy-start | bytes 4612
  31.9 5.5 %copy-start.16 = (f32[384]{0:T(512)S(1)}, f32[384]{0:T(512)}, u32[]{:S(2)}) copy-start(f32[384]{0:T(512)} %param.40) | copy-start | bytes 4612
  32.0 5.5 %copy-start.9 = (bf16[384,8]{0,1:T(8,128)(2,1)S(1)}, bf16[384,8]{0,1:T(8,128)(2,1)}, u32[]{:S(2)}) copy-start(bf16[384,8]{0,1:T(8,128)(2,1)} %param.41) | copy-start | bytes 18436
  32.0 6.3 %copy-start.7 = (f32[8,197,8]{1,2,0:T(8,128)S(1)}, f32[8,197,8]{1,2,0:T(8,128)}, u32[]{:S(2)}) copy-start(f32[8,197,8]{1,2,0:T(8,128)} %param.27) | copy-start | bytes 151300
  32.0 41.8 %all-to-all-start = ((bf16[8,400,384]{2,1,0:T(8,128)(2,1)}), bf16[8,400,384]{2,1,0:T(8,128)(2,1)S(1)}, u32[]{:S(2)}, u32[]{:S(2)}) async-start(bf16[8,400,384]{2,1,0:T(8,128)(2,1)} %get-tuple-element.52), calls=%async_computation | async-start | bytes 4915200 | tf_op jit(solution)/shard_map/all_to_all | solution.py:508
  73.8 34.9 %copy-start = (bf16[8,400,384]{2,1,0:T(8,128)(2,1)}, bf16[8,400,384]{2,1,0:T(8,128)(2,1)S(1)}, u32[]{:S(2)}) copy-start(bf16[8,400,384]{2,1,0:T(8,128)(2,1)S(1)} %all-to-all-done.g_ref) | copy-start | bytes 7372804
  138.4 34.1 %all-to-all-start.3 = ((bf16[8,400,384]{2,1,0:T(8,128)(2,1)}), bf16[8,400,384]{2,1,0:T(8,128)(2,1)S(1)}, u32[]{:S(2)}, u32[]{:S(2)}) async-start(bf16[8,400,384]{2,1,0:T(8,128)(2,1)} %get-tuple-element.62), calls=%async_computation.3 | async-start | bytes 4915200 | tf_op jit(solution)/shard_map/all_to_all | solution.py:560
  142.0 121.7 %reduce-scatter.5.cloned.1.call-start = ((), (), s32[]{:S(2)}) async-start(), calls=%async_computation.10 | async-start | bytes 1474560 | tf_op jit(solution)/shard_map/reduce_scatter | solution.py:579
  172.5 94.3 %reduce-scatter.3.cloned.1.call-start = ((), (), s32[]{:S(2)}) async-start(), calls=%async_computation.8 | async-start | bytes 1474560 | tf_op jit(solution)/shard_map/reduce_scatter | solution.py:578
  173.3 144.8 %all-gather.4.cloned.1.call-start = ((), (), s32[]{:S(2)}) async-start(), calls=%async_computation.7 | async-start | bytes 1437696 | tf_op jit(solution)/shard_map/all_gather | solution.py:473
  242.4 8.3 %collective-permute-start.2 = (bf16[208,384]{1,0:T(8,128)(2,1)S(1)}, bf16[208,384]{1,0:T(8,128)(2,1)S(1)}, u32[]{:S(2)}, u32[]{:S(2)}) collective-permute-start(bf16[208,384]{1,0:T(8,128)(2,1)S(1)} %reduce_sum.12), channel_id=1, source_target_pairs={{0,24},{8,0},{16,8},{24,16},{1,25},{9,1},{17,9},{25,17},{2,26},{10... | collective-permute-start | bytes 479240 | tf_op jit(solution)/shard_map/ppermute | solution.py:467
  246.1 13.0 %collective-permute-start.1 = (bf16[208,384]{1,0:T(8,128)(2,1)S(1)}, bf16[208,384]{1,0:T(8,128)(2,1)S(1)}, u32[]{:S(2)}, u32[]{:S(2)}) collective-permute-start(bf16[208,384]{1,0:T(8,128)(2,1)S(1)} %reduce_sum.12), channel_id=1, source_target_pairs={{0,16},{8,24},{16,0},{24,8},{1,17},{9,25},{17,1},{25,9},{2,18},{10... | collective-permute-start | bytes 479240 | tf_op jit(solution)/shard_map/ppermute | solution.py:467
  246.1 13.0 %collective-permute-start = (bf16[208,384]{1,0:T(8,128)(2,1)S(1)}, bf16[208,384]{1,0:T(8,128)(2,1)S(1)}, u32[]{:S(2)}, u32[]{:S(2)}) collective-permute-start(bf16[208,384]{1,0:T(8,128)(2,1)S(1)} %reduce_sum.12), channel_id=1, source_target_pairs={{0,8},{8,16},{16,24},{24,0},{1,9},{9,17},{17,25},{25,1},{2,10},{10... | collective-permute-start | bytes 479240 | tf_op jit(solution)/shard_map/ppermute | solution.py:467
  259.9 3.9 %copy-start.6 = (f32[1,384,384]{2,1,0:T(8,128)S(1)}, f32[1,384,384]{2,1,0:T(8,128)}, u32[]{:S(2)}) copy-start(f32[1,384,384]{2,1,0:T(8,128)} %param.45) | copy-start | bytes 1769476
  259.9 39.3 %all-to-all-start.2 = ((bf16[8,400,384]{2,1,0:T(8,128)(2,1)}), bf16[8,400,384]{2,1,0:T(8,128)(2,1)S(1)}, u32[]{:S(2)}, u32[]{:S(2)}) async-start(bf16[8,400,384]{2,1,0:T(8,128)(2,1)} %get-tuple-element.55), calls=%async_computation.2 | async-start | bytes 4915200 | tf_op jit(solution)/shard_map/all_to_all | solution.py:580
  263.7 64.8 %all-gather.8.cloned.1.call-start = ((), (), s32[]{:S(2)}) async-start(), calls=%async_computation.11 | async-start | bytes 1474560 | tf_op jit(solution)/shard_map/all_gather | solution.py:627
  266.7 93.3 %all-gather.6.cloned.1.call-start = ((), (), s32[]{:S(2)}) async-start(), calls=%async_computation.9 | async-start | bytes 1474560 | tf_op jit(solution)/shard_map/all_gather | solution.py:626
  328.5 33.9 %copy-start.5 = (bf16[1,1536,384]{2,1,0:T(8,128)(2,1)S(1)}, bf16[1,1536,384]{2,1,0:T(8,128)(2,1)}, u32[]{:S(2)}) copy-start(bf16[1,1536,384]{2,1,0:T(8,128)(2,1)} %all-gather.8.cloned.1.call-done) | copy-start | bytes 3538948
  (4 other events, 7.3 us)
Sparse Core Ops, SparseCore 0:
  172.6 28.6 reduce-scatter.4
  204.2 27.8 reduce-scatter.2
Sparse Core Ops, SparseCore 1:
  260.0 32.4 all-gather.3
  294.5 34.0 all-gather.7
  330.6 29.4 all-gather.5
